TPU v7x, 512 devices: a whole 4x8x8 slice. The times are simulated.
512 devices in a mesh: gx: 32 (over y, z_lo, core), gy: 16 (over x, z_hi).
Axes of the slice: x: 4, y: 8, z: 8 (z_hi: 4, z_lo: 2; z = z_hi * 2 + z_lo), core: 2. Of those that a mesh axis runs over, the one named last changes fastest.
Arguments:
- field: bfloat16 [512, 256, 4, 64], P('gx', 'gy'), may hold values from -6 to 6
- first_kernel: bfloat16 [1728, 64], replicated, may hold values from -0.21875 to 0.21875
- second_kernel: bfloat16 [1728, 64], replicated, may hold values from -0.15625 to 0.15625
- cotangent: bfloat16 [512, 256, 4, 64], P('gx', 'gy'), may hold values from -6 to 6
- samples: int32 [32, 16, 256], P('gx', 'gy'), may hold values from 0 to 1023
Outputs:
- output: bfloat16 [512, 256, 4, 64], P('gx', 'gy')
- first_update: float32 [1728, 64], replicated
- second_update: float32 [1728, 64], replicated
All inputs are finite; a program needn't handle non-finite values.
Results may differ from a plain program's by a relative error of at most 0.0034.
Values may be sent and summed in bfloat16 or wider, within the bound.
A program may use at most 64 MiB of HBM per device.

v0:
```python
import jax
import jax.numpy as jnp
from jax import lax
from jax.sharding import PartitionSpec as P

NS_ITERS = 5


def with_halo(block, sides, width):
    for axis, dim in sides:
        count = lax.axis_size(axis)
        forward = [(i, i + 1) for i in range(count - 1)]
        backward = [(target, source) for source, target in forward]
        low = lax.ppermute(
            lax.slice_in_dim(block, block.shape[dim] - width, None, axis=dim), axis, forward
        )
        high = lax.ppermute(lax.slice_in_dim(block, 0, width, axis=dim), axis, backward)
        block = jnp.concatenate([low, block, high], axis=dim)
    return block


def patches(padded, row_index, ylen, zlen):
    slab = lax.dynamic_slice_in_dim(padded, row_index, 3, 0)
    pieces = [
        slab[first, second : second + ylen, third : third + zlen, :]
        for first in range(3)
        for second in range(3)
        for third in range(3)
    ]
    return jnp.concatenate(pieces, -1).reshape(ylen * zlen, -1)


def convolve(framed, kernel):
    padded = jnp.pad(framed, ((0, 0), (0, 0), (1, 1), (0, 0)))
    xlen = framed.shape[0] - 2
    ylen = framed.shape[1] - 2
    zlen = framed.shape[2]
    width = kernel.shape[1]

    def one_row(row_index):
        return jnp.dot(
            patches(padded, row_index, ylen, zlen), kernel, preferred_element_type=jnp.float32
        )

    result = lax.map(one_row, jnp.arange(xlen, dtype=jnp.int32))
    return result.reshape(xlen, ylen, zlen, width)


def kernel_grad(framed, grads):
    padded = jnp.pad(framed, ((0, 0), (0, 0), (1, 1), (0, 0)))
    xlen, ylen, zlen, width = grads.shape

    def add_row(row_index, total):
        block = lax.dynamic_index_in_dim(grads, row_index, 0, keepdims=False).reshape(
            ylen * zlen, width
        )
        return total + jnp.dot(
            patches(padded, row_index, ylen, zlen).T, block, preferred_element_type=jnp.float32
        )

    start = jnp.zeros((27 * framed.shape[3], width), jnp.float32)
    return lax.fori_loop(0, xlen, add_row, start)


def flip_kernel(kernel, width):
    blocks = kernel.reshape(3, 3, 3, width, width)[::-1, ::-1, ::-1]
    return jnp.transpose(blocks, (0, 1, 2, 4, 3)).reshape(27 * width, width)


def newton_inverse(factor):
    width = factor.shape[0]
    identity = jnp.eye(width, dtype=jnp.float32)
    matrix = factor + 0.1 * identity
    approx = identity / jnp.sqrt(jnp.sum(matrix * matrix))
    for step in range(NS_ITERS):
        inner = 2.0 * identity - jnp.dot(matrix, approx, precision=lax.Precision.HIGHEST)
        approx = jnp.dot(approx, inner, precision=lax.Precision.HIGHEST)
    return approx


def precondition(grad, left_inv, right_inv, width):
    blocks = grad.reshape(27, width, width)
    result = jnp.einsum(
        "ab,tbc,cd->tad", left_inv, blocks, right_inv, precision=lax.Precision.HIGHEST
    )
    return result.reshape(27 * width, width)


def local_gram(values, cells, count):
    width = values.shape[3]
    picked = jnp.take(values.reshape(-1, width), cells, axis=0)
    return jnp.dot(picked.T, picked, preferred_element_type=jnp.float32) / count


def layer_inverses(inputs, outputs, cells, count):
    left_gram, right_gram = lax.psum(
        (local_gram(inputs, cells, count), local_gram(outputs, cells, count)), ("gx", "gy")
    )
    return (newton_inverse(left_gram), newton_inverse(right_gram))


def local(field, first_kernel, second_kernel, cotangent, samples):
    width = field.shape[3]
    xlen, ylen, zlen = (field.shape[0], field.shape[1], field.shape[2])
    tiles = lax.axis_size("gx") * lax.axis_size("gy")
    count = jnp.float32(tiles * samples.shape[2])
    cells = samples.reshape(-1)
    scale = 1.0 / jnp.sqrt(jnp.float32(tiles * xlen * ylen * zlen))
    framed_field = with_halo(field, (("gx", 0), ("gy", 1)), 1)
    hidden_pre = convolve(framed_field, first_kernel)
    hidden = jax.nn.silu(hidden_pre).astype(jnp.bfloat16)
    framed_hidden = with_halo(hidden, (("gx", 0), ("gy", 1)), 1)
    output = (field.astype(jnp.float32) + convolve(framed_hidden, second_kernel)).astype(
        jnp.bfloat16
    )
    framed_cotangent = with_halo(cotangent, (("gx", 0), ("gy", 1)), 1)
    second_grad = kernel_grad(framed_hidden, cotangent) * scale
    second_left, second_right = layer_inverses(hidden, cotangent, cells, count)
    back = convolve(framed_cotangent, flip_kernel(second_kernel, width))
    sigma = jax.nn.sigmoid(hidden_pre)
    delta = (back * sigma * (1.0 + hidden_pre * (1.0 - sigma))).astype(jnp.bfloat16)
    first_grad = kernel_grad(framed_field, delta) * scale
    first_left, first_right = layer_inverses(field, delta, cells, count)
    second_total, first_total = lax.psum((second_grad, first_grad), ("gx", "gy"))
    first_update = precondition(first_total, first_left, first_right, width)
    second_update = precondition(second_total, second_left, second_right, width)
    return (output, first_update, second_update)


def solution(mesh):
    placed = (P("gx", "gy", None, None), P(), P(), P("gx", "gy", None, None), P("gx", "gy", None))
    return jax.shard_map(
        local,
        mesh=mesh,
        in_specs=placed,
        out_specs=(P("gx", "gy", None, None), P(), P()),
        check_vma=False,
    )
```

profile of v0, /device:TPU:1, one launch (start us, length us, event | category | flops | bytes accessed | tf_op | source)
XLA Modules:
  0.0 836.6 jit_solution(13182387417172492346)
XLA Ops:
  8.0 5.4 collective-permute-start
  13.4 4.7 collective-permute-start.1
  18.9 1.9 collective-permute-start.8
  20.8 2.4 collective-permute-start.9
  24.6 1.7 gather_fusion.3
  29.3 1.7 rev.3
  31.4 4.3 collective-permute-start.2
  37.9 7.3 collective-permute-start.10
  47.0 75.0 %while.58 = (s32[]{:T(128)}, f32[16,64,64]{2,1,0:T(8,128)S(1)}, s32[16]{0:T(128)S(1)}, bf16[18,18,6,64]{3,2,1,0:T(8,128)(2,1)S(1)}, bf16[1728,64]{0,1:T(8,128)(2...) while((s32[]{:T(128)}, f32[16,64,64]{2,1,0:T(8,128)S(1)}, s32[16]{0:T(128)S(1)}, ...), condition=%wide.region_1.2_spmd, body=%wide.region_0.1_spmd.sunk | while | flops 14155785 | bytes 1376475 | solution.py:45
  122.0 1.5 select_maximum_fusion
  125.0 96.4 %while.60 = (s32[]{:T(128)}, f32[16,64,64]{2,1,0:T(8,128)}, s32[16]{0:T(128)}, bf16[18,18,6,64]{3,2,1,0:T(8,128)(2,1)S(1)}, bf16[1728,64]{1,0:T(8,128)(2,1)S(1)}...) while((s32[]{:T(128)}, f32[16,64,64]{2,1,0:T(8,128)}, s32[16]{0:T(128)}, ...), condition=%wide.region_5.6_spmd, body=%wide.region_4.5_spmd.sunk | while | flops 14155785 | bytes 1360599 | solution.py:45
  221.4 1.5 fusion.20
  225.0 4.2 collective-permute-start.4
  229.2 1.9 collective-permute-start.5
  231.2 25.0 %while.61 = (s32[]{:T(128)}, f32[1728,64]{0,1:T(8,128)S(1)}, bf16[18,18,6,64]{3,2,1,0:T(8,128)(2,1)S(1)}, bf16[16,16,4,64]{3,2,1,0:T(4,128)(2,1)}, s32[]{:T(128)}, /*index=5*/s32[]{}, s32[]{:T(128)}, s32[]{}) while((s32[]{:T(128)}, f32[1728,64]{0,1:T(8,128)S(1)}, bf16[18,18,6,64]{3,2,1,0:T(8,128)(2,1)S(1)}, ...), condition=%wide.region_7.8_spmd.clone, body=%wide.region_6.7_spmd.clone.sunk | while | flops 14376967 | bytes 2015395 | solution.py:62
  258.0 5.8 collective-permute-start.6
  266.4 1.5 copy.15
  268.1 2.6 collective-permute-done.7
  271.2 25.0 %while.62 = (s32[]{:T(128)}, f32[1728,64]{0,1:T(8,128)S(1)}, bf16[18,18,6,64]{3,2,1,0:T(8,128)(2,1)S(1)}, bf16[16,16,4,64]{3,2,1,0:T(4,128)(2,1)}, s32[]{:T(128)}, /*index=5*/s32[]{}, s32[]{:T(128)}, s32[]{}) while((s32[]{:T(128)}, f32[1728,64]{0,1:T(8,128)S(1)}, bf16[18,18,6,64]{3,2,1,0:T(8,128)(2,1)S(1)}, ...), condition=%wide.region_14.16_spmd.clone, body=%wide.region_13.15_spmd.clone.sunk | while | flops 14376967 | bytes 2015395 | solution.py:62
  296.4 51.7 %while.59 = (s32[]{:T(128)}, f32[16,64,64]{2,1,0:T(8,128)S(1)}, s32[16]{0:T(128)S(1)}, bf16[18,18,6,64]{3,2,1,0:T(8,128)(2,1)S(1)}, bf16[1728,64]{0,1:T(8,128)(2...) while((s32[]{:T(128)}, f32[16,64,64]{2,1,0:T(8,128)S(1)}, s32[16]{0:T(128)S(1)}, ...), condition=%wide.region_3.4_spmd, body=%wide.region_2.3_spmd.sunk | while | flops 14155785 | bytes 1376475 | solution.py:45
  350.9 191.8 %all-reduce.8.cloned.1.call-done = (f32[64,64]{1,0:T(8,128)}, f32[64,64]{1,0:T(8,128)}, f32[64,64]{1,0:T(8,128)}, f32[64,64]{1,0:T(8,128)}) async-done(((f32[64,64]{1,0:T(8,128)}, f32[64,64]{1,0:T(8,128)}, f32[64,64]{1,0:T(8,128)}, f32[64,64]{1,0:T(8,128)}), (f32[64,64]{1,0:T(8,128)}, f32[64,64]{1,0:T(8,128)}, f32[64,64]{1,0:T(8,128)}, f32[64,64]{1,0:T(8,128)})) %all-reduce.8.cloned.1.call-update) | async-done | bytes 65552 | tf_op jit(solution)/shard_map/psum | solution.py:96
  558.9 261.1 %all-reduce.10.cloned.1.call-done = (f32[27,64,64]{1,2,0:T(8,128)}, f32[27,64,64]{1,2,0:T(8,128)}) async-done(((f32[27,64,64]{1,2,0:T(8,128)}, f32[27,64,64]{1,2,0:T(8,128)}), (f32[27,64,64]{1,2,0:T(8,128)}, f32[27,64,64]{1,2,0:T(8,128)})) %all-reduce.10.cloned.1.call-update) | async-done | bytes 884752 | tf_op jit(solution)/shard_map/psum | solution.py:124
  820.0 3.5 fusion.125
  825.5 2.4 fusion.117
  (427 shorter events, 216.1 us)
Async XLA Ops:
  7.2 19.2 %copy-start.5 = (bf16[16,16,4,64]{3,2,1,0:T(4,128)(2,1)S(1)}, bf16[16,16,4,64]{3,2,1,0:T(4,128)(2,1)}, u32[]{:S(2)}) copy-start(bf16[16,16,4,64]{3,2,1,0:T(4,128)(2,1)} %param.17) | copy-start | bytes 393220
  7.2 21.8 %copy-start = (bf16[1728,64]{0,1:T(8,128)(2,1)S(1)}, bf16[1728,64]{0,1:T(8,128)(2,1)}, u32[]{:S(2)}) copy-start(bf16[1728,64]{0,1:T(8,128)(2,1)} %param.19) | copy-start | bytes 663556
  7.2 535.5 %all-reduce.8.cloned.1.call-start = ((), (), s32[]{:S(2)}) async-start(), calls=%async_computation | async-start | bytes 262144 | tf_op jit(solution)/shard_map/psum | solution.py:96
  8.0 23.1 %collective-permute-start = (bf16[1,16,4,64]{3,2,1,0:T(4,128)(2,1)S(1)}, bf16[1,16,4,64]{3,2,1,0:T(4,128)(2,1)S(1)}, u32[]{:S(2)}, u32[]{:S(2)}) collective-permute-start(bf16[1,16,4,64]{3,2,1,0:T(4,128)(2,1)S(1)} %get-tuple-element.496), channel_id=1, source_target_pairs={{0,16},{16,32},{32,48},{48,64},{64,80},{80,96},{96,112},{112,128},... | collective-permute-start | bytes 24584 | tf_op jit(solution)/shard_map/ppermute | solution.py:14
  13.4 17.9 %collective-permute-start.1 = (bf16[1,16,4,64]{3,2,1,0:T(4,128)(2,1)S(1)}, bf16[1,16,4,64]{3,2,1,0:T(4,128)(2,1)S(1)}, u32[]{:S(2)}, u32[]{:S(2)}) collective-permute-start(bf16[1,16,4,64]{3,2,1,0:T(4,128)(2,1)S(1)} %get-tuple-element.495), channel_id=1, source_target_pairs={{16,0},{32,16},{48,32},{64,48},{80,64},{96,80},{112,96},{128,112},... | collective-permute-start | bytes 24584 | tf_op jit(solution)/shard_map/ppermute | solution.py:17
  18.9 18.1 %collective-permute-start.8 = (bf16[1,16,4,64]{3,2,1,0:T(4,128)(2,1)S(1)}, bf16[1,16,4,64]{3,2,1,0:T(4,128)(2,1)S(1)}, u32[]{:S(2)}, u32[]{:S(2)}) collective-permute-start(bf16[1,16,4,64]{3,2,1,0:T(4,128)(2,1)S(1)} %get-tuple-element.492), channel_id=1, source_target_pairs={{0,16},{16,32},{32,48},{48,64},{64,80},{80,96},{96,112},{112,128},... | collective-permute-start | bytes 24584 | tf_op jit(solution)/shard_map/ppermute | solution.py:14
  20.8 16.3 %collective-permute-start.9 = (bf16[1,16,4,64]{3,2,1,0:T(4,128)(2,1)S(1)}, bf16[1,16,4,64]{3,2,1,0:T(4,128)(2,1)S(1)}, u32[]{:S(2)}, u32[]{:S(2)}) collective-permute-start(bf16[1,16,4,64]{3,2,1,0:T(4,128)(2,1)S(1)} %get-tuple-element.491), channel_id=1, source_target_pairs={{16,0},{32,16},{48,32},{64,48},{80,64},{96,80},{112,96},{128,112},... | collective-permute-start | bytes 24584 | tf_op jit(solution)/shard_map/ppermute | solution.py:17
  31.0 6.0 copy-start.7
  31.4 15.1 %collective-permute-start.2 = (bf16[18,1,4,64]{3,2,1,0:T(4,128)(2,1)S(1)}, bf16[18,1,4,64]{3,2,1,0:T(4,128)(2,1)S(1)}, u32[]{:S(2)}, u32[]{:S(2)}) collective-permute-start(bf16[18,1,4,64]{3,2,1,0:T(4,128)(2,1)S(1)} %get-tuple-element.489), channel_id=1, source_target_pairs={{0,1},{1,2},{2,3},{3,4},{4,5},{5,6},{6,7},{7,8},{8,9},{9,10},{10,1... | collective-permute-start | bytes 27656 | tf_op jit(solution)/shard_map/ppermute | solution.py:14
  35.7 10.9 %collective-permute-start.3 = (bf16[18,1,4,64]{3,2,1,0:T(4,128)(2,1)S(1)}, bf16[18,1,4,64]{3,2,1,0:T(4,128)(2,1)S(1)}, u32[]{:S(2)}, u32[]{:S(2)}) collective-permute-start(bf16[18,1,4,64]{3,2,1,0:T(4,128)(2,1)S(1)} %get-tuple-element.490), channel_id=1, source_target_pairs={{1,0},{2,1},{3,2},{4,3},{5,4},{6,5},{7,6},{8,7},{9,8},{10,9},{11,1... | collective-permute-start | bytes 27656 | tf_op jit(solution)/shard_map/ppermute | solution.py:17
  37.0 10.0 %copy-start.1 = (bf16[1728,64]{0,1:T(8,128)(2,1)S(1)}, bf16[1728,64]{0,1:T(8,128)(2,1)}, u32[]{:S(2)}) copy-start(bf16[1728,64]{0,1:T(8,128)(2,1)} %param.18) | copy-start | bytes 663556
  37.2 9.7 %copy-start.12 = (bf16[18,16,4,64]{3,2,1,0:T(4,128)(2,1)}, bf16[18,16,4,64]{3,2,1,0:T(4,128)(2,1)S(1)}, u32[]{:S(2)}) copy-start(bf16[18,16,4,64]{3,2,1,0:T(4,128)(2,1)S(1)} %constant_dynamic-update-slice_fusion.3) | copy-start | bytes 442372
  37.9 84.1 %collective-permute-start.10 = (bf16[18,1,4,64]{3,2,1,0:T(4,128)(2,1)}, bf16[18,1,4,64]{3,2,1,0:T(4,128)(2,1)}, u32[]{:S(2)}, u32[]{:S(2)}) collective-permute-start(bf16[18,1,4,64]{3,2,1,0:T(4,128)(2,1)} %get-tuple-element.485), channel_id=1, source_target_pairs={{0,1},{1,2},{2,3},{3,4},{4,5},{5,6},{6,7},{7,8},{8,9},{9,10},{10,1... | collective-permute-start | bytes 27656 | tf_op jit(solution)/shard_map/ppermute | solution.py:14
  45.2 76.8 %collective-permute-start.11 = (bf16[18,1,4,64]{3,2,1,0:T(4,128)(2,1)}, bf16[18,1,4,64]{3,2,1,0:T(4,128)(2,1)}, u32[]{:S(2)}, u32[]{:S(2)}) collective-permute-start(bf16[18,1,4,64]{3,2,1,0:T(4,128)(2,1)} %get-tuple-element.486), channel_id=1, source_target_pairs={{1,0},{2,1},{3,2},{4,3},{5,4},{6,5},{7,6},{8,7},{9,8},{10,9},{11,1... | collective-permute-start | bytes 27656 | tf_op jit(solution)/shard_map/ppermute | solution.py:17
  225.0 33.0 %collective-permute-start.4 = (bf16[1,16,4,64]{3,2,1,0:T(4,128)(2,1)S(1)}, bf16[1,16,4,64]{3,2,1,0:T(4,128)(2,1)S(1)}, u32[]{:S(2)}, u32[]{:S(2)}) collective-permute-start(bf16[1,16,4,64]{3,2,1,0:T(4,128)(2,1)S(1)} %get-tuple-element.493), channel_id=1, source_target_pairs={{0,16},{16,32},{32,48},{48,64},{64,80},{80,96},{96,112},{112,128},... | collective-permute-start | bytes 24584 | tf_op jit(solution)/shard_map/ppermute | solution.py:14
  229.2 28.8 %collective-permute-start.5 = (bf16[1,16,4,64]{3,2,1,0:T(4,128)(2,1)S(1)}, bf16[1,16,4,64]{3,2,1,0:T(4,128)(2,1)S(1)}, u32[]{:S(2)}, u32[]{:S(2)}) collective-permute-start(bf16[1,16,4,64]{3,2,1,0:T(4,128)(2,1)S(1)} %get-tuple-element.494), channel_id=1, source_target_pairs={{16,0},{32,16},{48,32},{64,48},{80,64},{96,80},{112,96},{128,112},... | collective-permute-start | bytes 24584 | tf_op jit(solution)/shard_map/ppermute | solution.py:17
  231.1 25.1 %copy-start.16 = (pred[256]{0:T(512)(128)(4,1)S(1)}, pred[256]{0:T(512)(128)(4,1)}, u32[]{:S(2)}) copy-start(pred[256]{0:T(512)(128)(4,1)} %copy-done.15) | copy-start | bytes 772
  258.0 10.1 %collective-permute-start.6 = (bf16[18,1,4,64]{3,2,1,0:T(4,128)(2,1)S(1)}, bf16[18,1,4,64]{3,2,1,0:T(4,128)(2,1)S(1)}, u32[]{:S(2)}, u32[]{:S(2)}) collective-permute-start(bf16[18,1,4,64]{3,2,1,0:T(4,128)(2,1)S(1)} %get-tuple-element.487), channel_id=1, source_target_pairs={{0,1},{1,2},{2,3},{3,4},{4,5},{5,6},{6,7},{7,8},{8,9},{9,10},{10,1... | collective-permute-start | bytes 27656 | tf_op jit(solution)/shard_map/ppermute | solution.py:14
  263.8 6.9 collective-permute-start.7
  267.9 552.1 %all-reduce.10.cloned.1.call-start = ((), (), s32[]{:S(2)}) async-start(), calls=%async_computation.1 | async-start | bytes 3538944 | tf_op jit(solution)/shard_map/psum | solution.py:124
  296.3 51.8 %copy-start.6 = (bf16[16,16,4,64]{3,2,1,0:T(4,128)(2,1)S(1)}, bf16[16,16,4,64]{3,2,1,0:T(4,128)(2,1)}, u32[]{:S(2)}) copy-start(bf16[16,16,4,64]{3,2,1,0:T(4,128)(2,1)} %param.17) | copy-start | bytes 393220
  542.7 9.4 %copy-start.11 = (f32[64,64]{1,0:T(8,128)S(1)}, f32[64,64]{1,0:T(8,128)}, u32[]{:S(2)}) copy-start(f32[64,64]{1,0:T(8,128)} %get-tuple-element.340) | copy-start | bytes 49156
  542.7 10.8 %copy-start.9 = (f32[64,64]{1,0:T(8,128)S(1)}, f32[64,64]{1,0:T(8,128)}, u32[]{:S(2)}) copy-start(f32[64,64]{1,0:T(8,128)} %get-tuple-element.338) | copy-start | bytes 49156
  542.7 10.8 %copy-start.10 = (f32[64,64]{1,0:T(8,128)S(1)}, f32[64,64]{1,0:T(8,128)}, u32[]{:S(2)}) copy-start(f32[64,64]{1,0:T(8,128)} %get-tuple-element.339) | copy-start | bytes 49156
  (7 other events, 19.6 us)
Sparse Core Ops, SparseCore 0:
  268.0 274.6 all-reduce.7
  548.6 271.3 all-reduce.9
where the time goes:
time: 845 us; the launch traced here: 837 us
  waiting for transfers between devices  456 us (54%)
  local copies, waits for them, and re-layouts  165 us (20%)
  loops' own time  95.5 us (11%)
  matrix products  51.6 us (6%)
  starting transfers between devices  42.1 us (5%)
  between operations  17.7 us (2%)
  other arithmetic  9.56 us (1%)
    psum x1, waiting for transfers between devices, local(): lax.psum((second_grad, first_grad), ('gx', 'gy'))  261 us
    psum x1, waiting for transfers between devices, layer_inverses(): lax.psum((local_gram(inputs, cells, count), local_gram(outputs, cells, co...  192 us
    another operation x3, loops' own time, convolve(): result = lax.map(one_row, jnp.arange(xlen, dtype=jnp.int32))  94.1 us
    slice x80, local copies, waits for them, and re-layouts, patches(): slab[first, second:second + ylen, third:third + zlen, :]  68.1 us
    concatenate x80, local copies, waits for them, and re-layouts, patches(): return jnp.concatenate(pieces, -1).reshape(ylen * zlen, -1)  41.4 us
    dynamic_slice x48, local copies, waits for them, and re-layouts, convolve(): result = lax.map(one_row, jnp.arange(xlen, dtype=jnp.int32))  38.6 us
    ppermute x6, starting transfers between devices, with_halo(): lax.ppermute(lax.slice_in_dim(block, block.shape[dim] - width, None, axis...  28.9 us
    dot_general x48, matrix products, one_row(): jnp.dot(patches(padded, row_index, ylen, zlen), kernel, preferred_element...  19.9 us
  transfers between devices with their start and end apart: 14, of which 3 were waited for; matrix products, arithmetic and copies ran while one was open for 17% of the time, Pallas kernels for 0%

commit v1 on v0

--- a/solution.py
+++ b/solution.py
@@ -94,7 +94,10 @@
 
 def layer_inverses(inputs, outputs, cells, count):
     left_gram, right_gram = lax.psum(
-        (local_gram(inputs, cells, count), local_gram(outputs, cells, count)), ("gx", "gy")
+        lax.psum(
+            (local_gram(inputs, cells, count), local_gram(outputs, cells, count)), axis_name="gy"
+        ),
+        axis_name="gx",
     )
     return (newton_inverse(left_gram), newton_inverse(right_gram))
 

time: 845 us -> 966 us (1.14)
  waiting for transfers between devices: 456 us -> 577 us
    psum x0 -> x1, waiting for transfers between devices: none -> 216 us  [layer_inverses(): lax.psum(lax.psum((local_gram(inputs, cells, count), local_gram(outputs,...]
    psum x1, waiting for transfers between devices: 192 us -> 90.6 us  [layer_inverses(): lax.psum((local_gram(inputs, cells, count), local_gram(outputs, cells, co...]
  transfers between devices with their start and end apart: 14 -> 15, of which waited for: 3 -> 4; matrix products, arithmetic and copies ran while one was open for 17% -> 15% of each run, Pallas kernels for 0% -> 0%
where the time goes in v1:
time: 966 us; the launch traced here: 958 us
  waiting for transfers between devices  577 us (60%)
  local copies, waits for them, and re-layouts  168 us (17%)
  loops' own time  91.4 us (9%)
  matrix products  51.8 us (5%)
  starting transfers between devices  42.1 us (4%)
  between operations  17.4 us (2%)
  other arithmetic  10.1 us (1%)
    psum x1, waiting for transfers between devices, local(): lax.psum((second_grad, first_grad), ('gx', 'gy'))  267 us
    psum x1, waiting for transfers between devices, layer_inverses(): lax.psum(lax.psum((local_gram(inputs, cells, count), local_gram(outputs,...  216 us
    psum x1, waiting for transfers between devices, layer_inverses(): lax.psum((local_gram(inputs, cells, count), local_gram(outputs, cells, co...  90.6 us
    another operation x3, loops' own time, convolve(): result = lax.map(one_row, jnp.arange(xlen, dtype=jnp.int32))  90 us
    slice x80, local copies, waits for them, and re-layouts, patches(): slab[first, second:second + ylen, third:third + zlen, :]  69.4 us
    concatenate x80, local copies, waits for them, and re-layouts, patches(): return jnp.concatenate(pieces, -1).reshape(ylen * zlen, -1)  43.1 us
    dynamic_slice x48, local copies, waits for them, and re-layouts, convolve(): result = lax.map(one_row, jnp.arange(xlen, dtype=jnp.int32))  38.1 us
    ppermute x6, starting transfers between devices, with_halo(): lax.ppermute(lax.slice_in_dim(block, block.shape[dim] - width, None, axis...  28.9 us
  transfers between devices with their start and end apart: 15, of which 4 were waited for; matrix products, arithmetic and copies ran while one was open for 15% of the time, Pallas kernels for 0%

profile of v1, /device:TPU:1, one launch (start us, length us, event | category | flops | bytes accessed | tf_op | source)
XLA Modules:
  0.0 957.7 jit_solution(17429839297407273004)
XLA Ops:
  8.0 5.4 collective-permute-start
  13.4 4.7 collective-permute-start.1
  18.9 1.9 collective-permute-start.8
  20.8 2.4 collective-permute-start.9
  24.6 1.7 gather_fusion.3
  29.3 1.7 rev.3
  31.4 4.3 collective-permute-start.2
  37.8 7.3 collective-permute-start.10
  47.0 72.8 %while.58 = (s32[]{:T(128)}, f32[16,64,64]{2,1,0:T(8,128)S(1)}, s32[16]{0:T(128)S(1)}, bf16[18,18,6,64]{3,2,1,0:T(8,128)(2,1)S(1)}, bf16[1728,64]{0,1:T(8,128)(2...) while((s32[]{:T(128)}, f32[16,64,64]{2,1,0:T(8,128)S(1)}, s32[16]{0:T(128)S(1)}, ...), condition=%wide.region_1.2_spmd, body=%wide.region_0.1_spmd.sunk | while | flops 14155785 | bytes 1376475 | solution.py:45
  123.4 96.7 %while.60 = (s32[]{:T(128)}, f32[16,64,64]{2,1,0:T(8,128)}, s32[16]{0:T(128)}, bf16[18,18,6,64]{3,2,1,0:T(8,128)(2,1)S(1)}, bf16[1728,64]{1,0:T(8,128)(2,1)S(1)}...) while((s32[]{:T(128)}, f32[16,64,64]{2,1,0:T(8,128)}, s32[16]{0:T(128)}, ...), condition=%wide.region_5.6_spmd, body=%wide.region_4.5_spmd.sunk | while | flops 14155785 | bytes 1360599 | solution.py:45
  220.1 2.2 fusion.20
  224.4 4.2 collective-permute-start.4
  228.7 1.9 collective-permute-start.5
  230.6 25.0 %while.61 = (s32[]{:T(128)}, f32[1728,64]{0,1:T(8,128)S(1)}, bf16[18,18,6,64]{3,2,1,0:T(8,128)(2,1)S(1)}, bf16[16,16,4,64]{3,2,1,0:T(4,128)(2,1)}, s32[]{:T(128)}, /*index=5*/s32[]{}, s32[]{:T(128)}, s32[]{}) while((s32[]{:T(128)}, f32[1728,64]{0,1:T(8,128)S(1)}, bf16[18,18,6,64]{3,2,1,0:T(8,128)(2,1)S(1)}, ...), condition=%wide.region_7.8_spmd.clone, body=%wide.region_6.7_spmd.clone.sunk | while | flops 14376967 | bytes 2015395 | solution.py:62
  257.5 5.8 collective-permute-start.6
  267.4 2.8 collective-permute-done.7
  270.7 25.1 %while.62 = (s32[]{:T(128)}, f32[1728,64]{0,1:T(8,128)S(1)}, bf16[18,18,6,64]{3,2,1,0:T(8,128)(2,1)S(1)}, bf16[16,16,4,64]{3,2,1,0:T(4,128)(2,1)}, s32[]{:T(128)}, /*index=5*/s32[]{}, s32[]{:T(128)}, s32[]{}) while((s32[]{:T(128)}, f32[1728,64]{0,1:T(8,128)S(1)}, bf16[18,18,6,64]{3,2,1,0:T(8,128)(2,1)S(1)}, ...), condition=%wide.region_16.18_spmd.clone, body=%wide.region_15.17_spmd.clone.sunk | while | flops 14376967 | bytes 2015395 | solution.py:62
  295.8 52.1 %while.59 = (s32[]{:T(128)}, f32[16,64,64]{2,1,0:T(8,128)S(1)}, s32[16]{0:T(128)S(1)}, bf16[18,18,6,64]{3,2,1,0:T(8,128)(2,1)S(1)}, bf16[1728,64]{0,1:T(8,128)(2...) while((s32[]{:T(128)}, f32[16,64,64]{2,1,0:T(8,128)S(1)}, s32[16]{0:T(128)S(1)}, ...), condition=%wide.region_3.4_spmd, body=%wide.region_2.3_spmd.sunk | while | flops 14155785 | bytes 1376475 | solution.py:45
  348.0 90.6 %all-reduce.14.cloned.1.call-done = (f32[64,64]{1,0:T(8,128)}, f32[64,64]{1,0:T(8,128)}, f32[64,64]{1,0:T(8,128)}, f32[64,64]{1,0:T(8,128)}) async-done(((f32[64,64]{1,0:T(8,128)}, f32[64,64]{1,0:T(8,128)}, f32[64,64]{1,0:T(8,128)}, f32[64,64]{1,0:T(8,128)}), (f32[64,64]{1,0:T(8,128)}, f32[64,64]{1,0:T(8,128)}, f32[64,64]{1,0:T(8,128)}, f32[64,64]{1,0:T(8,128)})) %all-reduce.14.cloned.1.call-update) | async-done | bytes 65552 | tf_op jit(solution)/shard_map/psum | solution.py:97
  440.1 1.5 copy.17
  441.6 216.4 %all-reduce.12.cloned.1.call-done = (f32[64,64]{1,0:T(8,128)}, f32[64,64]{1,0:T(8,128)}, f32[64,64]{1,0:T(8,128)}, f32[64,64]{1,0:T(8,128)}) async-done(((f32[64,64]{1,0:T(8,128)}, f32[64,64]{1,0:T(8,128)}, f32[64,64]{1,0:T(8,128)}, f32[64,64]{1,0:T(8,128)}), (f32[64,64]{1,0:T(8,128)}, f32[64,64]{1,0:T(8,128)}, f32[64,64]{1,0:T(8,128)}, f32[64,64]{1,0:T(8,128)})) %all-reduce.12.cloned.1.call-update) | async-done | bytes 65552 | tf_op jit(solution)/shard_map/psum | solution.py:96
  674.2 267.2 %all-reduce.10.cloned.1.call-done = (f32[27,64,64]{1,2,0:T(8,128)}, f32[27,64,64]{1,2,0:T(8,128)}) async-done(((f32[27,64,64]{1,2,0:T(8,128)}, f32[27,64,64]{1,2,0:T(8,128)}), (f32[27,64,64]{1,2,0:T(8,128)}, f32[27,64,64]{1,2,0:T(8,128)})) %all-reduce.10.cloned.1.call-update) | async-done | bytes 884752 | tf_op jit(solution)/shard_map/psum | solution.py:127
  941.4 3.5 fusion.125
  946.9 2.4 fusion.117
  (430 shorter events, 221.1 us)
Async XLA Ops:
  7.2 19.2 %copy-start.5 = (bf16[16,16,4,64]{3,2,1,0:T(4,128)(2,1)S(1)}, bf16[16,16,4,64]{3,2,1,0:T(4,128)(2,1)}, u32[]{:S(2)}) copy-start(bf16[16,16,4,64]{3,2,1,0:T(4,128)(2,1)} %param.17) | copy-start | bytes 393220
  7.2 21.8 %copy-start = (bf16[1728,64]{0,1:T(8,128)(2,1)S(1)}, bf16[1728,64]{0,1:T(8,128)(2,1)}, u32[]{:S(2)}) copy-start(bf16[1728,64]{0,1:T(8,128)(2,1)} %param.19) | copy-start | bytes 663556
  7.2 431.4 %all-reduce.14.cloned.1.call-start = ((), (), s32[]{:S(2)}) async-start(), calls=%async_computation.2 | async-start | bytes 262144 | tf_op jit(solution)/shard_map/psum | solution.py:97
  8.0 23.1 %collective-permute-start = (bf16[1,16,4,64]{3,2,1,0:T(4,128)(2,1)S(1)}, bf16[1,16,4,64]{3,2,1,0:T(4,128)(2,1)S(1)}, u32[]{:S(2)}, u32[]{:S(2)}) collective-permute-start(bf16[1,16,4,64]{3,2,1,0:T(4,128)(2,1)S(1)} %get-tuple-element.500), channel_id=1, source_target_pairs={{0,16},{16,32},{32,48},{48,64},{64,80},{80,96},{96,112},{112,128},... | collective-permute-start | bytes 24584 | tf_op jit(solution)/shard_map/ppermute | solution.py:14
  13.4 17.9 %collective-permute-start.1 = (bf16[1,16,4,64]{3,2,1,0:T(4,128)(2,1)S(1)}, bf16[1,16,4,64]{3,2,1,0:T(4,128)(2,1)S(1)}, u32[]{:S(2)}, u32[]{:S(2)}) collective-permute-start(bf16[1,16,4,64]{3,2,1,0:T(4,128)(2,1)S(1)} %get-tuple-element.499), channel_id=1, source_target_pairs={{16,0},{32,16},{48,32},{64,48},{80,64},{96,80},{112,96},{128,112},... | collective-permute-start | bytes 24584 | tf_op jit(solution)/shard_map/ppermute | solution.py:17
  18.9 18.1 %collective-permute-start.8 = (bf16[1,16,4,64]{3,2,1,0:T(4,128)(2,1)S(1)}, bf16[1,16,4,64]{3,2,1,0:T(4,128)(2,1)S(1)}, u32[]{:S(2)}, u32[]{:S(2)}) collective-permute-start(bf16[1,16,4,64]{3,2,1,0:T(4,128)(2,1)S(1)} %get-tuple-element.496), channel_id=1, source_target_pairs={{0,16},{16,32},{32,48},{48,64},{64,80},{80,96},{96,112},{112,128},... | collective-permute-start | bytes 24584 | tf_op jit(solution)/shard_map/ppermute | solution.py:14
  20.8 16.3 %collective-permute-start.9 = (bf16[1,16,4,64]{3,2,1,0:T(4,128)(2,1)S(1)}, bf16[1,16,4,64]{3,2,1,0:T(4,128)(2,1)S(1)}, u32[]{:S(2)}, u32[]{:S(2)}) collective-permute-start(bf16[1,16,4,64]{3,2,1,0:T(4,128)(2,1)S(1)} %get-tuple-element.495), channel_id=1, source_target_pairs={{16,0},{32,16},{48,32},{64,48},{80,64},{96,80},{112,96},{128,112},... | collective-permute-start | bytes 24584 | tf_op jit(solution)/shard_map/ppermute | solution.py:17
  31.0 6.0 copy-start.6
  31.4 15.1 %collective-permute-start.2 = (bf16[18,1,4,64]{3,2,1,0:T(4,128)(2,1)S(1)}, bf16[18,1,4,64]{3,2,1,0:T(4,128)(2,1)S(1)}, u32[]{:S(2)}, u32[]{:S(2)}) collective-permute-start(bf16[18,1,4,64]{3,2,1,0:T(4,128)(2,1)S(1)} %get-tuple-element.493), channel_id=1, source_target_pairs={{0,1},{1,2},{2,3},{3,4},{4,5},{5,6},{6,7},{7,8},{8,9},{9,10},{10,1... | collective-permute-start | bytes 27656 | tf_op jit(solution)/shard_map/ppermute | solution.py:14
  35.6 10.8 %collective-permute-start.3 = (bf16[18,1,4,64]{3,2,1,0:T(4,128)(2,1)S(1)}, bf16[18,1,4,64]{3,2,1,0:T(4,128)(2,1)S(1)}, u32[]{:S(2)}, u32[]{:S(2)}) collective-permute-start(bf16[18,1,4,64]{3,2,1,0:T(4,128)(2,1)S(1)} %get-tuple-element.494), channel_id=1, source_target_pairs={{1,0},{2,1},{3,2},{4,3},{5,4},{6,5},{7,6},{8,7},{9,8},{10,9},{11,1... | collective-permute-start | bytes 27656 | tf_op jit(solution)/shard_map/ppermute | solution.py:17
  37.0 10.0 %copy-start.1 = (bf16[1728,64]{0,1:T(8,128)(2,1)S(1)}, bf16[1728,64]{0,1:T(8,128)(2,1)}, u32[]{:S(2)}) copy-start(bf16[1728,64]{0,1:T(8,128)(2,1)} %param.18) | copy-start | bytes 663556
  37.2 9.3 copy-start.12
  37.8 82.0 %collective-permute-start.10 = (bf16[18,1,4,64]{3,2,1,0:T(4,128)(2,1)}, bf16[18,1,4,64]{3,2,1,0:T(4,128)(2,1)}, u32[]{:S(2)}, u32[]{:S(2)}) collective-permute-start(bf16[18,1,4,64]{3,2,1,0:T(4,128)(2,1)} %get-tuple-element.489), channel_id=1, source_target_pairs={{0,1},{1,2},{2,3},{3,4},{4,5},{5,6},{6,7},{7,8},{8,9},{9,10},{10,1... | collective-permute-start | bytes 27656 | tf_op jit(solution)/shard_map/ppermute | solution.py:14
  45.2 75.4 %collective-permute-start.11 = (bf16[18,1,4,64]{3,2,1,0:T(4,128)(2,1)}, bf16[18,1,4,64]{3,2,1,0:T(4,128)(2,1)}, u32[]{:S(2)}, u32[]{:S(2)}) collective-permute-start(bf16[18,1,4,64]{3,2,1,0:T(4,128)(2,1)} %get-tuple-element.490), channel_id=1, source_target_pairs={{1,0},{2,1},{3,2},{4,3},{5,4},{6,5},{7,6},{8,7},{9,8},{10,9},{11,1... | collective-permute-start | bytes 27656 | tf_op jit(solution)/shard_map/ppermute | solution.py:17
  224.4 33.0 %collective-permute-start.4 = (bf16[1,16,4,64]{3,2,1,0:T(4,128)(2,1)S(1)}, bf16[1,16,4,64]{3,2,1,0:T(4,128)(2,1)S(1)}, u32[]{:S(2)}, u32[]{:S(2)}) collective-permute-start(bf16[1,16,4,64]{3,2,1,0:T(4,128)(2,1)S(1)} %get-tuple-element.497), channel_id=1, source_target_pairs={{0,16},{16,32},{32,48},{48,64},{64,80},{80,96},{96,112},{112,128},... | collective-permute-start | bytes 24584 | tf_op jit(solution)/shard_map/ppermute | solution.py:14
  228.7 28.8 %collective-permute-start.5 = (bf16[1,16,4,64]{3,2,1,0:T(4,128)(2,1)S(1)}, bf16[1,16,4,64]{3,2,1,0:T(4,128)(2,1)S(1)}, u32[]{:S(2)}, u32[]{:S(2)}) collective-permute-start(bf16[1,16,4,64]{3,2,1,0:T(4,128)(2,1)S(1)} %get-tuple-element.498), channel_id=1, source_target_pairs={{16,0},{32,16},{48,32},{64,48},{80,64},{96,80},{112,96},{128,112},... | collective-permute-start | bytes 24584 | tf_op jit(solution)/shard_map/ppermute | solution.py:17
  230.6 25.1 %copy-start.16 = (pred[256]{0:T(512)(128)(4,1)S(1)}, pred[256]{0:T(512)(128)(4,1)}, u32[]{:S(2)}) copy-start(pred[256]{0:T(512)(128)(4,1)} %copy-done.15) | copy-start | bytes 772
  257.5 9.9 %collective-permute-start.6 = (bf16[18,1,4,64]{3,2,1,0:T(4,128)(2,1)S(1)}, bf16[18,1,4,64]{3,2,1,0:T(4,128)(2,1)S(1)}, u32[]{:S(2)}, u32[]{:S(2)}) collective-permute-start(bf16[18,1,4,64]{3,2,1,0:T(4,128)(2,1)S(1)} %get-tuple-element.491), channel_id=1, source_target_pairs={{0,1},{1,2},{2,3},{3,4},{4,5},{5,6},{6,7},{7,8},{8,9},{9,10},{10,1... | collective-permute-start | bytes 27656 | tf_op jit(solution)/shard_map/ppermute | solution.py:14
  263.3 6.9 collective-permute-start.7
  267.4 390.6 %all-reduce.12.cloned.1.call-start = ((), (), s32[]{:S(2)}) async-start(), calls=%async_computation.1 | async-start | bytes 262144 | tf_op jit(solution)/shard_map/psum | solution.py:96
  438.6 502.8 %all-reduce.10.cloned.1.call-start = ((), (), s32[]{:S(2)}) async-start(), calls=%async_computation | async-start | bytes 3538944 | tf_op jit(solution)/shard_map/psum | solution.py:127
  658.0 9.4 copy-start.11
  658.0 10.8 %copy-start.9 = (f32[64,64]{1,0:T(8,128)S(1)}, f32[64,64]{1,0:T(8,128)}, u32[]{:S(2)}) copy-start(f32[64,64]{1,0:T(8,128)} %get-tuple-element.340) | copy-start | bytes 49156
  658.0 10.8 %copy-start.10 = (f32[64,64]{1,0:T(8,128)S(1)}, f32[64,64]{1,0:T(8,128)}, u32[]{:S(2)}) copy-start(f32[64,64]{1,0:T(8,128)} %get-tuple-element.341) | copy-start | bytes 49156
  (8 other events, 20.4 us)
Sparse Core Ops, SparseCore 0:
  267.5 171.0 all-reduce.13
  442.1 215.8 all-reduce.11
  663.1 278.2 all-reduce.9
